TPU v7x, 512 devices: a whole 4x4x16 slice. The times are simulated.
512 devices in a mesh: batch: 16 (over y, x), group: 32 (over z, core).
Axes of the slice: x: 4, y: 4, z: 16, core: 2. Of those that a mesh axis runs over, the one named last changes fastest.
Arguments:
- noise: bfloat16 [2048, 99840], P('batch', 'group'), may hold values from -24 to 24
- data: bfloat16 [2048, 99840], P('batch', 'group'), may hold values from -6 to 6
Outputs:
- targets: bfloat16 [2048, 99840], P('batch', 'group')
- potential: float32 [2048], replicated
All inputs are finite; a program needn't handle non-finite values.
Results may differ from a plain program's by a relative error of at most 0.007.
Values may be sent and summed in bfloat16 or wider, within the bound.
A program may use at most 64 MiB of HBM per device.

v0:
```python
import jax
import jax.numpy as jnp
from jax import lax
from jax.sharding import PartitionSpec as P

ITERS = 4
FEAT = 99840


def combined_all(value, axis, join):
    pieces = jax.tree.map(lambda part: lax.all_gather(part, axis), value)
    head = jax.tree.map(lambda part: part[0], pieces)
    tail = jax.tree.map(lambda part: part[1:], pieces)
    total, _ = lax.scan(lambda total, slab: (join(total, slab), None), head, tail)
    return total


def combine_parts(first, second):
    top = jnp.maximum(first[0], second[0])
    total = first[1] * jnp.exp(first[0] - top) + second[1] * jnp.exp(second[0] - top)
    return (top, total)


def local_parts(values, axis):
    top = jnp.max(values, axis=axis)
    total = jnp.sum(jnp.exp(values - jnp.expand_dims(top, axis)), axis=axis)
    return (top, total)


def local(noise, data):
    eps = 2.0 / jnp.sqrt(jnp.float32(FEAT))
    batch_total = noise.shape[0] * lax.axis_size("batch")
    loga = -jnp.log(jnp.float32(batch_total))
    noise_sq = jnp.sum(jnp.square(noise.astype(jnp.float32)), axis=1)
    all_rows = lax.all_gather(data, "batch", axis=0, tiled=True)
    piece_sq = jnp.sum(jnp.square(all_rows.astype(jnp.float32)), axis=1)
    cross = lax.dot_general(
        noise, all_rows, (((1,), (1,)), ((), ())), preferred_element_type=jnp.float32
    )
    partial_value = noise_sq[:, None] + piece_sq[None, :] - 2.0 * cross
    cost = lax.psum(partial_value, "group") / jnp.float32(FEAT)
    potential = jnp.zeros((batch_total,), jnp.float32)
    for step in range(ITERS):
        top, total = local_parts((potential[None, :] - cost) / eps, 1)
        rowpot = eps * loga - eps * (top + jnp.log(total))
        parts = local_parts((rowpot[:, None] - cost) / eps, 0)
        top, total = combined_all(parts, "batch", combine_parts)
        potential = eps * loga - eps * (top + jnp.log(total))
    scores = (potential[None, :] - cost) / eps
    top, total = local_parts(scores, 1)
    weights = jnp.exp(scores - (top + jnp.log(total))[:, None]).astype(jnp.bfloat16)
    targets = jnp.dot(weights, all_rows, preferred_element_type=jnp.float32)
    return (targets.astype(jnp.bfloat16), potential)


def solution(mesh):
    in_specs = (P("batch", "group"), P("batch", "group"))
    out_specs = (P("batch", "group"), P())
    return jax.shard_map(local, mesh=mesh, in_specs=in_specs, out_specs=out_specs, check_vma=False)
```

profile of v0, /device:TPU:24, one launch (start us, length us, event | category | flops | bytes accessed | tf_op | source)
XLA Modules:
  0.0 567.8 jit_solution(14642108242688481387)
XLA Ops:
  7.2 0.0 copy-start.1
  7.2 0.0 all-gather.10.cloned.1.call-start
  7.2 0.7 all-gather.10.cloned.1.call-update
  7.9 0.0 all-reduce.2.cloned.1.call-start
  8.0 1.6 multiply_reduce_fusion.1
  9.5 121.3 %all-gather.10.cloned.1.call-done = bf16[2048,3120]{0,1:T(8,128)(2,1)} async-done(((bf16[128,3120]{0,1:T(8,128)(2,1)}), bf16[2048,3120]{0,1:T(8,128)(2,1)}) %all-gather.10.cloned.1.call-update) | async-done | bytes 12779536 | tf_op jit(solution)/shard_map/all_gather | solution.py:35
  130.8 7.2 %multiply_reduce_fusion = f32[2048]{0:T(1024)S(1)} fusion(bf16[2048,3120]{0,1:T(8,128)(2,1)} %all-gather.10.cloned.1.call-done), kind=kLoop, calls=%fused_computation.12 | loop fusion | flops 19167232 | bytes 12787712 | tf_op jit(solution)/shard_map/reduce_sum | solution.py:36
  138.0 0.0 copy-done.1
  138.0 7.6 %fusion = f32[128,2048]{1,0:T(8,128)} fusion(bf16[128,3120]{0,1:T(8,128)(2,1)S(1)} %copy-done.1, bf16[2048,3120]{0,1:T(8,128)(2,1)} %all-gather.10.cloned.1.call-done, f32[2048]{0:T(1024)S(1)} %multiply_reduce_fusion, f32[128]{0:T(128)S(1)} %multiply_reduce_fusion.1), kind=kOutput, calls=%fused_computation.15 | convolution fusion | flops 1636564992 | bytes 14635520 | tf_op jit(solution)/shard_map/dot_general | solution.py:37
  145.6 0.0 all-reduce.2.cloned.1.call-update
  145.6 210.2 %all-reduce.2.cloned.1.call-done = f32[128,2048]{1,0:T(8,128)} async-done(((f32[128,2048]{1,0:T(8,128)}), f32[128,2048]{1,0:T(8,128)}) %all-reduce.2.cloned.1.call-update) | async-done | bytes 1048592 | tf_op jit(solution)/shard_map/psum | solution.py:41
  355.8 0.0 copy-start
  355.8 1.5 fusion.1
  357.4 1.6 exponential_reduce_fusion.8
  359.0 1.4 fusion.2
  360.4 23.3 %all-gather = f32[32768]{0:T(1024)S(1)} all-gather(f32[2048]{0:T(1024)S(1)} %fusion.2), channel_id=2, replica_groups=mesh['batch'=16,'group'=32] {'batch'}, dimensions={0}, use_global_device_ids=true | all-gather | bytes 139264 | tf_op jit(solution)/shard_map/all_gather | solution.py:11
  383.7 1.5 exponential_reduce_fusion.7
  385.2 21.4 %all-gather.1 = f32[32768]{0:T(1024)S(1)} all-gather(f32[2048]{0:T(1024)S(1)} %exponential_reduce_fusion.7), channel_id=3, replica_groups=mesh['batch'=16,'group'=32] {'batch'}, dimensions={0}, use_global_device_ids=true | all-gather | bytes 139264 | tf_op jit(solution)/shard_map/all_gather | solution.py:11
  406.8 0.9 while.48
  407.7 1.5 fusion.3
  409.2 1.6 exponential_reduce_fusion.6
  410.8 1.4 fusion.4
  412.2 23.0 %all-gather.2 = f32[32768]{0:T(1024)S(1)} all-gather(f32[2048]{0:T(1024)S(1)} %fusion.4), channel_id=4, replica_groups=mesh['batch'=16,'group'=32] {'batch'}, dimensions={0}, use_global_device_ids=true | all-gather | bytes 139264 | tf_op jit(solution)/shard_map/all_gather | solution.py:11
  435.2 1.5 exponential_reduce_fusion.5
  436.7 21.4 %all-gather.3 = f32[32768]{0:T(1024)S(1)} all-gather(f32[2048]{0:T(1024)S(1)} %exponential_reduce_fusion.5), channel_id=5, replica_groups=mesh['batch'=16,'group'=32] {'batch'}, dimensions={0}, use_global_device_ids=true | all-gather | bytes 139264 | tf_op jit(solution)/shard_map/all_gather | solution.py:11
  458.3 0.9 while.49
  459.2 0.0 copy-done
  459.2 0.2 fusion.5
  459.5 0.4 exponential_reduce_fusion.4
  459.8 0.2 fusion.6
  460.1 23.0 %all-gather.4 = f32[32768]{0:T(1024)S(1)} all-gather(f32[2048]{0:T(1024)S(1)} %fusion.6), channel_id=6, replica_groups=mesh['batch'=16,'group'=32] {'batch'}, dimensions={0}, use_global_device_ids=true | all-gather | bytes 139264 | tf_op jit(solution)/shard_map/all_gather | solution.py:11
  483.0 0.3 exponential_reduce_fusion.3
  483.4 21.4 %all-gather.5 = f32[32768]{0:T(1024)S(1)} all-gather(f32[2048]{0:T(1024)S(1)} %exponential_reduce_fusion.3), channel_id=7, replica_groups=mesh['batch'=16,'group'=32] {'batch'}, dimensions={0}, use_global_device_ids=true | all-gather | bytes 139264 | tf_op jit(solution)/shard_map/all_gather | solution.py:11
  504.9 0.9 while.50
  505.9 0.2 fusion.7
  506.1 0.4 exponential_reduce_fusion.2
  506.5 0.2 fusion.8
  506.7 23.1 %all-gather.6 = f32[32768]{0:T(1024)S(1)} all-gather(f32[2048]{0:T(1024)S(1)} %fusion.8), channel_id=8, replica_groups=mesh['batch'=16,'group'=32] {'batch'}, dimensions={0}, use_global_device_ids=true | all-gather | bytes 139264 | tf_op jit(solution)/shard_map/all_gather | solution.py:11
  529.8 0.3 exponential_reduce_fusion.1
  530.1 21.4 %all-gather.7 = f32[32768]{0:T(1024)S(1)} all-gather(f32[2048]{0:T(1024)S(1)} %exponential_reduce_fusion.1), channel_id=9, replica_groups=mesh['batch'=16,'group'=32] {'batch'}, dimensions={0}, use_global_device_ids=true | all-gather | bytes 139264 | tf_op jit(solution)/shard_map/all_gather | solution.py:11
  551.7 0.9 while.51
  552.7 0.0 copy-start.2
  552.7 0.2 fusion.9
  552.9 0.4 exponential_reduce_fusion
  553.3 7.6 %convolution_convert_fusion = bf16[128,3120]{0,1:T(8,128)(2,1)} fusion(bf16[2048,3120]{0,1:T(8,128)(2,1)} %all-gather.10.cloned.1.call-done, f32[128]{0:T(128)S(1)} %log_add_fusion, f32[2048]{0:T(1024)S(1)} %multiply_subtract_fusion, f32[128,2048]{1,0:T(8,128)S(1)} %copy-done), kind=kOutput, calls=%fused_computation.13 | convolution fusion | flops 1637488640 | bytes 14635520 | tf_op jit(solution)/shard_map/dot_general | solution.py:52
  560.9 0.0 copy-done.2
  (153 shorter events, 2.3 us)
Async XLA Ops:
  7.2 130.9 %copy-start.1 = (bf16[128,3120]{0,1:T(8,128)(2,1)S(1)}, bf16[128,3120]{0,1:T(8,128)(2,1)}, u32[]{:S(2)}) copy-start(bf16[128,3120]{0,1:T(8,128)(2,1)} %param.10) | copy-start | bytes 2396164
  7.2 123.7 %all-gather.10.cloned.1.call-start = ((), (), s32[]{:S(2)}) async-start(), calls=%async_computation | async-start | bytes 13578240 | tf_op jit(solution)/shard_map/all_gather | solution.py:35
  7.9 347.9 %all-reduce.2.cloned.1.call-start = ((), (), s32[]{:S(2)}) async-start(), calls=%async_computation.1 | async-start | bytes 2097152 | tf_op jit(solution)/shard_map/psum | solution.py:41
  355.8 103.4 %copy-start = (f32[128,2048]{1,0:T(8,128)S(1)}, f32[128,2048]{1,0:T(8,128)}, u32[]{:S(2)}) copy-start(f32[128,2048]{1,0:T(8,128)} %all-reduce.2.cloned.1.call-done) | copy-start | bytes 3145732
  552.7 8.2 %copy-start.2 = (f32[2048]{0:T(1024)}, f32[2048]{0:T(1024)S(1)}, u32[]{:S(2)}) copy-start(f32[2048]{0:T(1024)S(1)} %multiply_subtract_fusion) | copy-start | bytes 24580
Sparse Core Ops, SparseCore 0:
  11.0 119.7 all-gather.9
  145.7 210.0 all-reduce.1
where the time goes:
time: 569 us; the launch traced here: 568 us
  waiting for transfers between devices  332 us (58%)
  blocking collectives  178 us (31%)
  other arithmetic  24.6 us (4%)
  matrix products  15.2 us (3%)
  between operations  14.4 us (3%)
    psum x1, waiting for transfers between devices, local(): cost = lax.psum(partial_value, 'group') / jnp.float32(FEAT)  210 us
    all_gather x8, blocking collectives, combined_all(): pieces = jax.tree.map(lambda part: lax.all_gather(part, axis), value)  178 us
    all_gather x1, waiting for transfers between devices, local(): all_rows = lax.all_gather(data, 'batch', axis=0, tiled=True)  121 us
  transfers between devices with their start and end apart: 2, of which 2 were waited for; matrix products, arithmetic and copies ran while one was open for 0% of the time, Pallas kernels for 0%

commit v1 on v0

v1 whole, which is shorter than its diff:
```python
import jax
import jax.numpy as jnp
import numpy as np
from jax import lax
from jax.experimental import pallas as pl
from jax.experimental.pallas import tpu as pltpu
from jax.sharding import PartitionSpec as P

MESH = pl.DeviceIdType.MESH
ITERS = 4
FEAT = 99840
BATCH = 2048
ROWS = 128
WIDE = 3120
PAD = 3200
TAIL = WIDE // 128 * 128
EPS = np.float32(2.0 / np.sqrt(np.float32(FEAT)))
LOGA = np.float32(-np.log(np.float32(BATCH)))
SCALE = np.float32(2.0 / (np.float64(FEAT) * np.float64(EPS)))
A_ROWS = 80
A_CUT = 48
N_SEM = 160
TILE = 640


def split3(value):
    high = value.astype(jnp.bfloat16).astype(jnp.float32)
    rest = value - high
    mid = rest.astype(jnp.bfloat16).astype(jnp.float32)
    return high, mid, rest - mid


def offset_of(s):
    return s + (s // 2) * (1 - 2 * (s % 2))


def pack(src_ref, store, own_parts, own_at, const, const_at):
    total = jnp.zeros((ROWS, 1), jnp.float32)
    for at in range(0, WIDE, 640):
        cut = slice(at, min(at + 640, WIDE))
        piece = src_ref[:, cut].astype(jnp.float32)
        total = total + jnp.sum(piece * piece, axis=1, keepdims=True)
    parts = split3(total * own_parts)
    lane = lax.broadcasted_iota(jnp.int32, (ROWS, PAD - TAIL), 1)
    extra = jnp.zeros((ROWS, PAD - TAIL), jnp.float32)
    for k, part in enumerate(parts):
        extra = jnp.where(lane == WIDE - TAIL + own_at + k, part, extra)
        extra = jnp.where(lane == WIDE - TAIL + const_at + k, jnp.float32(const), extra)
    store(extra.astype(jnp.bfloat16), lane)


def kernel(
    noise_ref, data_ref, out_ref, pot_ref,
    D, Nb, C, R0, R1, S1, R2, F, M, L, lbuf, pbuf, W, tail, send, recv,
):
    b = lax.axis_index("batch")
    g = lax.axis_index("group")
    y, x, z, c = b // 4, b % 4, g // 2, g % 2
    rho, s = z % 4, z // 4

    def dev(dy=0, dx=0, dz=0, dc=0):
        return (((y + dy) % 4) * 4 + (x + dx) % 4, ((z + dz) % 16) * 2 + (c + dc) % 2)

    right, left, up, down, sibling = dev(dx=1), dev(dx=3), dev(dy=1), dev(dy=3), dev(dc=1)
    count = [0]
    started = []

    def make(src, dst, device):
        k = count[0]
        count[0] += 1
        return pltpu.make_async_remote_copy(src, dst, send.at[k], recv.at[k], device_id=device, device_id_type=MESH)

    def go(src, dst, device):
        copy = make(src, dst, device)
        copy.start()
        started.append(copy)
        return copy

    near = [(dy, dx, 0, 0) for dy in range(4) for dx in range(4) if (dy, dx) != (0, 0)]
    far = [(0, 0, dz, 0) for dz in (1, 2, 14, 15)] + [(0, dx, dz, 0) for dx in range(4) for dz in (4, 8, 12)]
    peers = near + far + [(0, 0, 0, 1)]
    barrier = pltpu.get_barrier_semaphore()
    for peer in peers:
        pl.semaphore_signal(barrier, inc=1, device_id=dev(*peer), device_id_type=MESH)

    def rows(x_, y_, first=0, n=ROWS):
        return pl.ds(pl.multiple_of((x_ * 4 + y_) * ROWS + first, 16), n)

    def blk(x_, y_, first=0, n=ROWS):
        return D.at[rows(x_, y_, first, n)]

    own = rows(x, y)

    def place(ref, dst, where):
        dst[where, 0:TAIL] = ref[:, 0:TAIL]
        tail[:, 0 : WIDE - TAIL] = ref[:, TAIL:WIDE]

        def store(extra, lane):
            dst[where, TAIL:PAD] = jnp.where(lane < WIDE - TAIL, tail[...], extra)

        return store

    tail[...] = jnp.zeros_like(tail)
    pack(noise_ref, place(noise_ref, Nb, slice(0, ROWS)), -0.5, 0, -0.5, 3)
    pack(data_ref, place(data_ref, D, own), 1.0, 3, 1.0, 0)

    pl.semaphore_wait(barrier, len(peers))

    h = ROWS // 2

    def nb(i, first, n):
        return Nb.at[pl.ds(i * ROWS + first, n)]

    n_r0 = go(nb(0, 0, h), nb(2, 0, h), right)
    n_l0 = go(nb(0, h, h), nb(1, h, h), left)
    d_u0 = go(blk(x, y, 0, h), blk(x, y, 0, h), up)
    d_d0 = go(blk(x, y, h, h), blk(x, y, h, h), down)
    n_r1 = go(nb(0, h, h), nb(2, h, h), right)
    n_l1 = go(nb(0, 0, h), nb(1, 0, h), left)
    d_u1 = go(blk(x, y, h, h), blk(x, y, h, h), up)
    d_d1 = go(blk(x, y, 0, h), blk(x, y, 0, h), down)
    xr, xl, xo = (x + 1) % 4, (x + 3) % 4, (x + 2) % 4
    yu, yd, yo = (y + 1) % 4, (y + 3) % 4, (y + 2) % 4
    n_r0.wait_recv()
    n_ro = go(nb(2, 0, h), nb(3, 0, h), right)
    n_l0.wait_recv()
    n_lo = go(nb(1, h, h), nb(3, h, h), left)
    d_u0.wait_recv()
    d_uo = go(blk(x, yd, 0, h), blk(x, yd, 0, h), up)
    d_d0.wait_recv()
    d_do = go(blk(x, yu, h, h), blk(x, yu, h, h), down)

    nB = ROWS - A_ROWS
    a_r = go(blk(x, y, 0, A_ROWS), blk(x, y, 0, A_ROWS), right)
    a_l = go(blk(x, y, 0, A_ROWS), blk(x, y, 0, A_ROWS), left)
    b_r, b_l = {}, {}

    def send_b(table, y_name, y_, device):
        table[y_name] = go(blk(x, y_, A_ROWS, nB), blk(x, y_, A_ROWS, nB), device)

    def nt(a, b_):
        return lax.dot_general(a, b_, (((1,), (1,)), ((), ())), preferred_element_type=jnp.float32)

    def cols(y_):
        return pl.ds(pl.multiple_of(y_ * ROWS, ROWS), ROWS)

    n_r1.wait_recv()
    n_l1.wait_recv()
    C[0 : 3 * ROWS, cols(y)] = nt(Nb[0 : 3 * ROWS], D[own])
    d_u1.wait_recv()
    d_d1.wait_recv()
    send_b(b_r, "y", y, right)
    send_b(b_l, "d", yd, left)
    for y_ in (yu, yd):
        C[0 : 3 * ROWS, cols(y_)] = nt(Nb[0 : 3 * ROWS], D[rows(x, y_)])
    d_uo.wait_recv()
    d_do.wait_recv()
    C[0 : 3 * ROWS, cols(yo)] = nt(Nb[0 : 3 * ROWS], D[rows(x, yo)])
    n_ro.wait_recv()
    n_lo.wait_recv()
    C[3 * ROWS :, :] = nt(Nb[3 * ROWS :], D[pl.ds(pl.multiple_of(x * 4 * ROWS, ROWS), 4 * ROWS)])

    def half(core, i):
        return pl.ds(pl.multiple_of(i * ROWS + core * h, h), h)

    cores = [go(C.at[half(1 - c, i)], R0.at[pl.ds(i * h, h)], sibling) for i in range(4)]

    def sixteen(at):
        return pl.ds(pl.multiple_of(at, 16), 16)

    dz2 = 2 - 4 * c + 16
    steps = [(1, dev(dz=1)), (3, dev(dz=15)), (2, dev(dz=dz2))]
    window = {}
    for i in range(4):
        cores[i].wait_recv()
        R0[i * h : (i + 1) * h] = R0[i * h : (i + 1) * h] + C[half(c, i)]
        for t, (dq, device) in enumerate(steps):
            window[i, t] = go(
                R0.at[sixteen(i * h + 16 * ((rho + dq) % 4))], R1.at[t, pl.ds(i * 16, 16)], device
            )
    send_b(b_r, "u", yu, right)
    send_b(b_l, "o", yo, left)
    for i in range(4):
        for t in range(3):
            window[i, t].wait_recv()
        S1[i * 16 : (i + 1) * 16] = (
            R0[sixteen(i * h + 16 * rho)] + R1[0, i * 16 : (i + 1) * 16]
            + (R1[1, i * 16 : (i + 1) * 16] + R1[2, i * 16 : (i + 1) * 16])
        )
    stride = {}
    for d in (2, 1, 3):
        stride[d] = go(S1.at[sixteen(16 * ((s + d) % 4))], R2.at[d - 1], dev(dz=4 * d))

    a_r.wait_recv()
    a_l.wait_recv()
    ao_r = go(blk(xl, y, 0, A_CUT), blk(xl, y, 0, A_CUT), right)
    ao_l = go(blk(xr, y, A_CUT, A_ROWS - A_CUT), blk(xr, y, A_CUT, A_ROWS - A_CUT), left)
    send_b(b_r, "d", yd, right)
    send_b(b_l, "y", y, left)
    a_u, a_d = {}, {}

    def send_a(name, x_):
        a_u[name] = go(blk(x_, y, 0, A_ROWS), blk(x_, y, 0, A_ROWS), up)
        a_d[name] = go(blk(x_, y, 0, A_ROWS), blk(x_, y, 0, A_ROWS), down)

    send_a("r", xr)
    send_a("l", xl)

    for d in (1, 2, 3):
        stride[d].wait_recv()
    F[...] = (S1[sixteen(16 * s)] + R2[0] + (R2[1] + R2[2])) * SCALE

    mine = sixteen(c * h + 16 * rho)

    def part(x_):
        return M.at[mine, pl.ds(pl.multiple_of(x_ * 512, 512), 512)]

    dx = offset_of(s)
    home = {}
    for d in (2, 1, 3):
        home[d] = go(F, part(x), dev(dx=dx, dz=4 * d))
    home[0] = make(F, part(x), dev(dx=dx))

    @pl.when(s != 0)
    def _():
        home[0].start()

    @pl.when(s == 0)
    def _():
        M[mine, pl.ds(pl.multiple_of(x * 512, 512), 512)] = F[...]

    def fwd_b_r(name, y_):
        b_r[name].wait_recv()
        return go(blk(xl, y_, A_ROWS, nB), blk(xl, y_, A_ROWS, nB), right)

    def fwd_b_l(name, y_):
        b_l[name].wait_recv()
        return go(blk(xr, y_, A_ROWS, nB), blk(xr, y_, A_ROWS, nB), left)

    late = []
    spread, pair = {}, []
    for d in (0, 1, 3, 2):
        if d == 0:

            @pl.when(s != 0)
            def _():
                home[0].wait_recv()

        else:
            home[d].wait_recv()
        region = part((x + 4 - offset_of((s + 4 - d) % 4)) % 4)
        for t, (_, device) in enumerate(steps):
            spread[d, t] = go(region, region, device)
        pair.append(go(region, region, sibling))

    late.append(fwd_b_r("y", y))
    late.append(fwd_b_l("d", yd))
    send_b(b_r, "o", yo, right)
    send_b(b_l, "u", yu, left)
    ao_r.wait_recv()
    ao_l.wait_recv()
    send_a("o", xo)

    for t, dq in ((0, 3), (1, 1), (2, 2)):
        for d in range(4):
            spread[d, t].wait_recv()
        region = M.at[sixteen(c * h + 16 * ((rho + dq) % 4))]
        pair.append(go(region, region, sibling))
    for copy in pair:
        copy.wait_recv()

    def fwd_a(name, x_):
        a_u[name].wait_recv()
        late.append(go(blk(x_, yd, 0, A_CUT), blk(x_, yd, 0, A_CUT), up))
        a_d[name].wait_recv()
        late.append(go(blk(x_, yu, A_CUT, A_ROWS - A_CUT), blk(x_, yu, A_CUT, A_ROWS - A_CUT), down))

    def between(step):
        if step == 0:
            fwd_a("r", xr)
            late.append(fwd_b_r("u", yu))
        if step == 1:
            fwd_a("l", xl)
            late.append(fwd_b_l("o", yo))
        if step == 2:
            fwd_a("o", xo)

    def block(k):
        return M[:, k * ROWS : (k + 1) * ROWS]

    def row_lse():
        top = block(0) + pbuf[0:1, :]
        for k in range(1, 16):
            top = jnp.maximum(top, block(k) + pbuf[k : k + 1, :])
        top = jnp.max(top, axis=1, keepdims=True)
        total = jnp.exp(block(0) + pbuf[0:1, :] - top)
        for k in range(1, 16):
            total = total + jnp.exp(block(k) + pbuf[k : k + 1, :] - top)
        return top + jnp.log(jnp.sum(total, axis=1, keepdims=True))

    pbuf[...] = jnp.zeros_like(pbuf)
    for step in range(ITERS):
        rowpot = LOGA - row_lse()
        for k in range(16):
            values = block(k) + rowpot
            top = jnp.max(values, axis=0, keepdims=True)
            total = jnp.sum(jnp.exp(values - top), axis=0, keepdims=True)
            lbuf[step, k : k + 1, :] = top + jnp.log(total)
        slot = pl.ds(pl.multiple_of(b * 16, 16), 16)
        L[step, slot] = lbuf[step]
        swaps = [go(lbuf.at[step], L.at[step, slot], dev(*peer)) for peer in near]
        between(step)
        for copy in swaps:
            copy.wait_recv()
        top = L[step, 0:16]
        for k in range(1, 16):
            top = jnp.maximum(top, L[step, k * 16 : (k + 1) * 16])
        total = jnp.exp(L[step, 0:16] - top)
        for k in range(1, 16):
            total = total + jnp.exp(L[step, k * 16 : (k + 1) * 16] - top)
        pbuf[...] = LOGA - (top + jnp.log(total))

    lse = row_lse()
    for k in range(16):
        W[:, k * ROWS : (k + 1) * ROWS] = jnp.exp(block(k) + pbuf[k : k + 1, :] - lse).astype(jnp.bfloat16)
        pot_ref[(k % 4) * 4 + k // 4 : (k % 4) * 4 + k // 4 + 1, :] = pbuf[k : k + 1, :] * EPS

    for name in ("d", "o"):
        b_r[name].wait_recv()
    for name in ("y", "u"):
        b_l[name].wait_recv()
    for copy in late:
        copy.wait_recv()
    for at in range(0, WIDE, TILE):
        cut = slice(at, min(at + TILE, WIDE))
        out_ref[:, cut] = jnp.dot(W[...], D[:, cut], preferred_element_type=jnp.float32).astype(jnp.bfloat16)

    for copy in started:
        copy.wait_send()

    @pl.when(s != 0)
    def _():
        home[0].wait_send()


def local(noise, data):
    f32, bf16 = jnp.float32, jnp.bfloat16
    vmem = pl.BlockSpec(memory_space=pltpu.VMEM)
    targets, potential = pl.pallas_call(
        kernel,
        name="pairing",
        out_shape=(jax.ShapeDtypeStruct((ROWS, WIDE), bf16), jax.ShapeDtypeStruct((16, ROWS), f32)),
        in_specs=[vmem] * 2,
        out_specs=(vmem, vmem),
        scratch_shapes=[
            pltpu.VMEM((BATCH, PAD), bf16),
            pltpu.VMEM((4 * ROWS, PAD), bf16),
            pltpu.VMEM((512, 512), f32),
            pltpu.VMEM((256, 512), f32),
            pltpu.VMEM((3, 64, 512), f32),
            pltpu.VMEM((64, 512), f32),
            pltpu.VMEM((3, 16, 512), f32),
            pltpu.VMEM((16, 512), f32),
            pltpu.VMEM((ROWS, BATCH), f32),
            pltpu.VMEM((ITERS, 256, 128), f32),
            pltpu.VMEM((ITERS, 16, 128), f32),
            pltpu.VMEM((16, 128), f32),
            pltpu.VMEM((ROWS, BATCH), bf16),
            pltpu.VMEM((ROWS, PAD - TAIL), bf16),
            pltpu.SemaphoreType.DMA((N_SEM,)),
            pltpu.SemaphoreType.DMA((N_SEM,)),
        ],
        compiler_params=pltpu.CompilerParams(
            collective_id=0, has_side_effects=True, vmem_limit_bytes=48 * 1024 * 1024
        ),
    )(noise, data)
    return targets, potential.reshape(BATCH)


def solution(mesh):
    in_specs = (P("batch", "group"), P("batch", "group"))
    out_specs = (P("batch", "group"), P())
    return jax.shard_map(local, mesh=mesh, in_specs=in_specs, out_specs=out_specs, check_vma=False)
```

time: 569 us -> 131 us (0.23)
  waiting for transfers between devices: 332 us -> 0 us
  blocking collectives: 178 us -> 0 us
  Pallas kernels: 0 us -> 124 us
  other arithmetic: 24.6 us -> 0 us
  matrix products: 15.2 us -> 0 us
  between operations: 14.4 us -> 0.67 us
    psum x1 -> x0, waiting for transfers between devices: 210 us -> none  [local(): cost = lax.psum(partial_value, 'group') / jnp.float32(FEAT)]
    all_gather x8 -> x0, blocking collectives: 178 us -> none  [combined_all(): pieces = jax.tree.map(lambda part: lax.all_gather(part, axis), value)]
    pallas_call x0 -> x1, Pallas kernels: none -> 124 us  [local(): pl.pallas_call(kernel, name='pairing', out_shape=(jax.ShapeDtypeStruct((R...]
    all_gather x1 -> x0, waiting for transfers between devices: 121 us -> none  [local(): all_rows = lax.all_gather(data, 'batch', axis=0, tiled=True)]
    reduce_sum x11 -> x0, other arithmetic: 16.7 us -> none  [the longest x9 7.93 us: local_parts(): total = jnp.sum(jnp.exp(values - jnp.expand_dims(top, axis)), axis=axis)]
    dot_general x2 -> x0, matrix products: 15.2 us -> none  [the longest x1 7.64 us: local(): targets = jnp.dot(weights, all_rows, preferred_element_type=jnp.float32)]
    reduce_max x9 -> x0, other arithmetic: 6.99 us -> none  [local_parts(): top = jnp.max(values, axis=axis)]
  transfers between devices with their start and end apart: 2 -> 0, of which waited for: 2 -> 0; matrix products, arithmetic and copies ran while one was open for 0% -> 0% of each run, Pallas kernels for 0% -> 0%
where the time goes in v1:
time: 131 us; the launch traced here: 130 us
  Pallas kernels  124 us (95%)
  local copies, waits for them, and re-layouts  4.61 us (4%)
    pallas_call x1, Pallas kernels, local(): pl.pallas_call(kernel, name='pairing', out_shape=(jax.ShapeDtypeStruct((R...  124 us
    unnamed x6, local copies, waits for them, and re-layouts  4.61 us

profile of v1, /device:TPU:24, one launch (start us, length us, event | category | flops | bytes accessed | tf_op | source)
XLA Modules:
  0.0 129.6 jit_solution(2436958764614208953)
XLA Ops:
  0.6 0.0 copy-start
  0.6 1.6 %copy.4.noise_ref = bf16[128,3120]{1,0:T(8,128)(2,1)S(1)} copy(bf16[128,3120]{0,1:T(8,128)(2,1)} %param.2) | data formatting | bytes 1597440 | tf_op args[0]
  2.3 0.0 copy-done
  2.3 1.1 copy.5.data_ref
  3.4 124.4 %pairing.1 = (bf16[128,3120]{1,0:T(8,128)(2,1)S(1)}, f32[16,128]{1,0:T(8,128)S(1)}) custom-call(bf16[128,3120]{1,0:T(8,128)(2,1)S(1)} %copy.4.noise_ref, bf16[128,3120]{1,0:T(8,128)(2,1)S(1)} %copy.5.data_ref), custom_call_target="tpu_custom_call" | custom-call | tf_op jit(solution)/shard_map/pairing/pallas_call | solution.py:349
  127.7 1.3 copy.6
  129.0 0.6 copy.8
Async XLA Ops:
  0.6 1.6 %copy-start = (bf16[128,3120]{0,1:T(8,128)(2,1)S(1)}, bf16[128,3120]{0,1:T(8,128)(2,1)}, u32[]{:S(2)}) copy-start(bf16[128,3120]{0,1:T(8,128)(2,1)} %param.3) | copy-start | bytes 2396164

commit v2 on v1

v2 whole, which is shorter than its diff:
```python
import jax
import jax.numpy as jnp
import numpy as np
from jax import lax
from jax.experimental import pallas as pl
from jax.experimental.pallas import tpu as pltpu
from jax.sharding import PartitionSpec as P

MESH = pl.DeviceIdType.MESH
ITERS = 4
FEAT = 99840
BATCH = 2048
ROWS = 128
WIDE = 3120
DEEP = WIDE + 16
EPS = np.float32(2.0 / np.sqrt(np.float32(FEAT)))
LOGA = np.float32(-np.log(np.float32(BATCH)))
SCALE = np.float32(2.0 / (np.float64(FEAT) * np.float64(EPS)))
A = ((0, 784), (784, 1168))
A_DEEP = 1952
B = ((1952, 400), (2352, 400), (2752, 384))
HALF = 1536
N_SEM = 224
TILE = 624


def split3(value):
    high = value.astype(jnp.bfloat16).astype(jnp.float32)
    rest = value - high
    mid = rest.astype(jnp.bfloat16).astype(jnp.float32)
    return high, mid, rest - mid


def offset_of(s):
    return s + (s // 2) * (1 - 2 * (s % 2))


def place(src_ref, dst, start, factor, own_at, const, const_at):
    def chunk(k, total):
        at = pl.multiple_of(k * 240, 16)
        piece = src_ref[pl.ds(at, 240)]
        dst[pl.ds(pl.multiple_of(start + at, 16), 240)] = piece
        piece = piece.astype(jnp.float32)
        return total + jnp.sum((piece * piece).reshape(30, 8, ROWS), axis=0)

    total = lax.fori_loop(0, WIDE // 240, chunk, jnp.zeros((8, ROWS), jnp.float32))
    parts = split3(jnp.sum(total, axis=0, keepdims=True) * factor)
    line = lax.broadcasted_iota(jnp.int32, (16, ROWS), 0)
    extra = jnp.zeros((16, ROWS), jnp.float32)
    for k, part in enumerate(parts):
        extra = jnp.where(line == own_at + k, part, extra)
        extra = jnp.where(line == const_at + k, jnp.float32(const), extra)
    dst[pl.ds(pl.multiple_of(start + WIDE, 16), 16)] = extra.astype(jnp.bfloat16)


def kernel(
    noise_ref, data_ref, out_ref, pot_ref,
    D, NT, Nr, C, R0, R1, S1, R2, F, M, L, lbuf, pbuf, W, known, send, recv,
):
    b = lax.axis_index("batch")
    g = lax.axis_index("group")
    y, x, z, c = b // 4, b % 4, g // 2, g % 2
    rho, s = z % 4, z // 4

    def dev(dy=0, dx=0, dz=0, dc=0):
        return (((y + dy) % 4) * 4 + (x + dx) % 4, ((z + dz) % 16) * 2 + (c + dc) % 2)

    right, left, up, down, sibling = dev(dx=1), dev(dx=3), dev(dy=1), dev(dy=3), dev(dc=1)
    count = [0]
    started = []

    def make(src, dst, device):
        k = count[0]
        count[0] += 1
        assert k < N_SEM
        return pltpu.make_async_remote_copy(src, dst, send.at[k], recv.at[k], device_id=device, device_id_type=MESH)

    def go(src, dst, device):
        copy = make(src, dst, device)
        copy.start()
        started.append(copy)
        return copy

    barrier = pltpu.get_barrier_semaphore()
    next_ones = (right, left, up, down, dev(dz=1), dev(dz=15), sibling)
    for device in next_ones:
        pl.semaphore_signal(barrier, inc=1, device_id=device, device_id_type=MESH)

    def tell(k, *devices):
        for device in devices:
            pl.semaphore_signal(known.at[k], inc=1, device_id=device, device_id_type=MESH)

    def hear(k, n=1):
        pl.semaphore_wait(known.at[k], n)

    def rows(x_, y_, first=0, n=DEEP):
        return pl.ds(pl.multiple_of((x_ * 4 + y_) * DEEP + first, 16), n)

    def blk(x_, y_, first=0, n=DEEP):
        return D.at[rows(x_, y_, first, n)]

    def nb(i, first, n):
        return NT.at[pl.ds(i * DEEP + first, n)]

    place(noise_ref, NT, 0, -0.5, 0, -0.5, 3)
    place(data_ref, D, (x * 4 + y) * DEEP, 1.0, 3, 1.0, 0)
    pl.semaphore_wait(barrier, len(next_ones))

    one, two = (0, HALF), (HALF, DEEP - HALF)
    n_r0 = go(nb(0, *one), nb(2, *one), right)
    n_l0 = go(nb(0, *two), nb(1, *two), left)
    d_u0 = go(blk(x, y, *one), blk(x, y, *one), up)
    d_d0 = go(blk(x, y, *two), blk(x, y, *two), down)
    n_r1 = go(nb(0, *two), nb(2, *two), right)
    n_l1 = go(nb(0, *one), nb(1, *one), left)
    d_u1 = go(blk(x, y, *two), blk(x, y, *two), up)
    d_d1 = go(blk(x, y, *one), blk(x, y, *one), down)
    xr, xl, xo = (x + 1) % 4, (x + 3) % 4, (x + 2) % 4
    yu, yd, yo = (y + 1) % 4, (y + 3) % 4, (y + 2) % 4
    tell(0, right)
    tell(1, up)
    tell(2, dev(dz=1))
    tell(3, dev(dz=15))

    def flip(i, part):
        first, n = part
        for at in range(first, first + n, ROWS):
            size = min(ROWS, first + n - at)
            Nr[i * ROWS : (i + 1) * ROWS, at : at + size] = NT[i * DEEP + at : i * DEEP + at + size, :].T

    flip(0, (0, DEEP))
    for k in range(4):
        hear(k)
    tell(4, dev(dz=2))
    tell(5, dev(dz=14))
    tell(6, up, down, dev(dy=2))
    n_r0.wait_recv()
    n_ro = go(nb(2, *one), nb(3, *one), right)
    n_l0.wait_recv()
    n_lo = go(nb(1, *two), nb(3, *two), left)
    d_u0.wait_recv()
    d_uo = go(blk(x, yd, *one), blk(x, yd, *one), up)
    d_d0.wait_recv()
    d_do = go(blk(x, yu, *two), blk(x, yu, *two), down)
    flip(2, one)
    flip(1, two)
    hear(4)
    hear(5)
    hear(6, 3)
    tell(7, dev(dz=4))

    a_r, a_l = {}, {}
    for piece in A:
        a_r[piece] = go(blk(x, y, *piece), blk(x, y, *piece), right)
        a_l[piece] = go(blk(x, y, *piece), blk(x, y, *piece), left)
    b_r, b_l = {}, {}

    def send_b(r_name, r_y, l_name, l_y, *pieces):
        for piece in pieces:
            b_r[r_name, piece] = go(blk(x, r_y, *piece), blk(x, r_y, *piece), right)
            b_l[l_name, piece] = go(blk(x, l_y, *piece), blk(x, l_y, *piece), left)

    a_u, a_d = {}, {}

    def send_a(name, x_, piece):
        a_u[name, piece] = go(blk(x_, y, *piece), blk(x_, y, *piece), up)
        a_d[name, piece] = go(blk(x_, y, *piece), blk(x_, y, *piece), down)

    def turn_a(piece):
        a_r[piece].wait_recv()
        a_l[piece].wait_recv()
        send_a("r", xr, piece)
        send_a("l", xl, piece)

    late = []

    def fwd_b(r_name, r_y, l_name, l_y, *pieces):
        for piece in pieces:
            b_r.pop((r_name, piece)).wait_recv()
            late.append(go(blk(xl, r_y, *piece), blk(xl, r_y, *piece), right))
            b_l.pop((l_name, piece)).wait_recv()
            late.append(go(blk(xr, l_y, *piece), blk(xr, l_y, *piece), left))

    def fwd_a(name, x_, piece):
        first, size = piece
        n = size // 32 * 16
        a_u[name, piece].wait_recv()
        late.append(go(blk(x_, yd, first, n), blk(x_, yd, first, n), up))
        a_d[name, piece].wait_recv()
        late.append(go(blk(x_, yu, first + n, size - n), blk(x_, yu, first + n, size - n), down))

    def cross(i, n, j, y_):
        C[i * ROWS : (i + n) * ROWS, j * ROWS : (j + 1) * ROWS] = jnp.dot(
            Nr[i * ROWS : (i + n) * ROWS, :], D[rows(x, y_)], preferred_element_type=jnp.float32
        )

    h = ROWS // 2

    def half(core, i):
        return pl.ds(pl.multiple_of(i * ROWS + core * h, h), h)

    def sixteen(at):
        return pl.ds(pl.multiple_of(at, 16), 16)

    steps = [(1, dev(dz=1)), (3, dev(dz=15)), (2, dev(dz=18 - 4 * c))]

    def to_core(blocks):
        copies = []
        for i, first, n, at in blocks:
            copy = go(C.at[half(1 - c, i), pl.ds(first, n)], R0.at[:, pl.ds(at, n)], sibling)
            copies.append((copy, half(c, i), first, n, at))
        return copies

    def to_window(copies, at, n):
        for copy, mine_, first, size, to in copies:
            copy.wait_recv()
            R0[:, to : to + size] = R0[:, to : to + size] + C[mine_, first : first + size]
        return [
            go(R0.at[sixteen(16 * ((rho + dq) % 4)), pl.ds(at, n)], R1.at[t, :, pl.ds(at, n)], device)
            for t, (dq, device) in enumerate(steps)
        ]

    def add_window(copies, blocks):
        for copy in copies:
            copy.wait_recv()
        for i, first, n, at in blocks:
            for k in range(0, n, ROWS):
                cut = slice(at + k, at + k + ROWS)
                y_ = (y, yu, yd, yo)[(first + k) // ROWS]
                S1[i * 16 : (i + 1) * 16, pl.ds(pl.multiple_of(y_ * ROWS, ROWS), ROWS)] = (
                    R0[sixteen(16 * rho), cut] + R1[0, :, cut] + (R1[1, :, cut] + R1[2, :, cut])
                )

    early = [(0, 0, 384, 0), (1, 0, 384, 384), (2, 0, 384, 768)]
    rest = [(0, 384, 128, 1152), (1, 384, 128, 1280), (2, 384, 128, 1408), (3, 0, 512, 1536)]

    n_r1.wait_recv()
    flip(2, two)
    n_l1.wait_recv()
    flip(1, one)
    cross(0, 3, 0, y)
    d_u1.wait_recv()
    d_d1.wait_recv()
    send_b("y", y, "d", yd, *B)
    cross(0, 3, 1, yu)
    cross(0, 3, 2, yd)
    early_core = to_core(early)
    early_window = to_window(early_core, 0, 1152)
    hear(7)
    tell(8, dev(dz=4), dev(dz=8), dev(dz=12))
    d_uo.wait_recv()
    d_do.wait_recv()
    cross(0, 3, 3, yo)
    n_ro.wait_recv()
    flip(3, one)
    n_lo.wait_recv()
    flip(3, two)
    for j, y_ in enumerate((y, yu, yd, yo)):
        cross(3, 1, j, y_)
    rest_core = to_core(rest)
    add_window(early_window, early)
    rest_window = to_window(rest_core, 1152, 896)
    turn_a(A[0])
    add_window(rest_window, rest)
    stride = {}
    for d in (2, 1, 3):
        stride[d] = go(S1.at[sixteen(16 * ((s + d) % 4))], R2.at[d - 1], dev(dz=4 * d))
    turn_a(A[1])
    ao_r = go(blk(xl, y, 0, A_DEEP // 2), blk(xl, y, 0, A_DEEP // 2), right)
    ao_l = go(blk(xr, y, A_DEEP // 2, A_DEEP // 2), blk(xr, y, A_DEEP // 2, A_DEEP // 2), left)
    hear(8, 3)
    for d in (1, 2, 3):
        stride[d].wait_recv()
    F[...] = (S1[sixteen(16 * s)] + R2[0] + (R2[1] + R2[2])) * SCALE

    mine = sixteen(c * h + 16 * rho)

    def part(x_):
        return M.at[mine, pl.ds(pl.multiple_of(x_ * 512, 512), 512)]

    dx = offset_of(s)
    home = {}
    for d in (2, 1, 3):
        home[d] = go(F, part(x), dev(dx=dx, dz=4 * d))
    home[0] = make(F, part(x), dev(dx=dx))

    @pl.when(s != 0)
    def _():
        home[0].start()

    @pl.when(s == 0)
    def _():
        M[mine, pl.ds(pl.multiple_of(x * 512, 512), 512)] = F[...]

    fwd_a("r", xr, A[0])
    fwd_a("l", xl, A[0])
    send_b("u", yu, "o", yo, *B)
    fwd_b("y", y, "d", yd, *B)
    spread, pair = {}, []
    for d in (0, 1, 3, 2):
        if d == 0:

            @pl.when(s != 0)
            def _():
                home[0].wait_recv()

        else:
            home[d].wait_recv()
        region = part((x + 4 - offset_of((s + 4 - d) % 4)) % 4)
        for t, (_, device) in enumerate(steps):
            spread[d, t] = go(region, region, device)
        pair.append(go(region, region, sibling))

    send_b("d", yd, "y", y, B[0])
    ao_r.wait_recv()
    ao_l.wait_recv()
    for piece in A:
        send_a("o", xo, piece)

    for t, dq in ((0, 3), (1, 1), (2, 2)):
        for d in range(4):
            spread[d, t].wait_recv()
        region = M.at[sixteen(c * h + 16 * ((rho + dq) % 4))]
        pair.append(go(region, region, sibling))
    for copy in pair:
        copy.wait_recv()

    def between(step):
        if step == 0:
            fwd_a("r", xr, A[1])
            send_b("d", yd, "y", y, *B[1:])
        if step == 1:
            fwd_a("l", xl, A[1])
            send_b("o", yo, "u", yu, *B[:2])
        if step == 2:
            fwd_a("o", xo, A[0])
            send_b("o", yo, "u", yu, B[2])
            fwd_b("u", yu, "o", yo, B[0])
        if step == 3:
            fwd_a("o", xo, A[1])
            fwd_b("u", yu, "o", yo, *B[1:])

    def block(k):
        return M[:, k * ROWS : (k + 1) * ROWS]

    def row_lse():
        top = block(0) + pbuf[0:1, :]
        for k in range(1, 16):
            top = jnp.maximum(top, block(k) + pbuf[k : k + 1, :])
        top = jnp.max(top, axis=1, keepdims=True)
        total = jnp.exp(block(0) + pbuf[0:1, :] - top)
        for k in range(1, 16):
            total = total + jnp.exp(block(k) + pbuf[k : k + 1, :] - top)
        return top + jnp.log(jnp.sum(total, axis=1, keepdims=True))

    near = [(dy, dx, 0, 0) for dy in range(4) for dx in range(4) if (dy, dx) != (0, 0)]
    near.sort(key=lambda peer: -min(peer[0], 4 - peer[0]) - min(peer[1], 4 - peer[1]))
    pbuf[...] = jnp.zeros_like(pbuf)
    for step in range(ITERS):
        rowpot = LOGA - row_lse()
        for k in range(16):
            values = block(k) + rowpot
            top = jnp.max(values, axis=0, keepdims=True)
            total = jnp.sum(jnp.exp(values - top), axis=0, keepdims=True)
            lbuf[step, k : k + 1, :] = top + jnp.log(total)
        slot = pl.ds(pl.multiple_of(b * 16, 16), 16)
        L[step, slot] = lbuf[step]
        swaps = [go(lbuf.at[step], L.at[step, slot], dev(*peer)) for peer in near]
        between(step)
        for copy in swaps:
            copy.wait_recv()
        top = L[step, 0:16]
        for k in range(1, 16):
            top = jnp.maximum(top, L[step, k * 16 : (k + 1) * 16])
        total = jnp.exp(L[step, 0:16] - top)
        for k in range(1, 16):
            total = total + jnp.exp(L[step, k * 16 : (k + 1) * 16] - top)
        pbuf[...] = LOGA - (top + jnp.log(total))

    lse = row_lse()
    for k in range(16):
        W[:, k * ROWS : (k + 1) * ROWS] = jnp.exp(block(k) + pbuf[k : k + 1, :] - lse).astype(jnp.bfloat16)
        pot_ref[(k % 4) * 4 + k // 4 : (k % 4) * 4 + k // 4 + 1, :] = pbuf[k : k + 1, :] * EPS

    for copy in [*b_r.values(), *b_l.values(), *late]:
        copy.wait_recv()
    for at in range(0, WIDE, TILE):
        all_rows = jnp.concatenate([D[k * DEEP + at : k * DEEP + at + TILE, :] for k in range(16)], axis=1)
        out_ref[at : at + TILE, :] = lax.dot_general(
            all_rows, W[...], (((1,), (1,)), ((), ())), preferred_element_type=jnp.float32
        ).astype(jnp.bfloat16)

    for copy in started:
        copy.wait_send()

    @pl.when(s != 0)
    def _():
        home[0].wait_send()


def local(noise, data):
    f32, bf16 = jnp.float32, jnp.bfloat16
    vmem = pl.BlockSpec(memory_space=pltpu.VMEM)
    targets, potential = pl.pallas_call(
        kernel,
        name="pairing",
        out_shape=(jax.ShapeDtypeStruct((WIDE, ROWS), bf16), jax.ShapeDtypeStruct((16, ROWS), f32)),
        in_specs=[vmem] * 2,
        out_specs=(vmem, vmem),
        scratch_shapes=[
            pltpu.VMEM((16 * DEEP, ROWS), bf16),
            pltpu.VMEM((4 * DEEP, ROWS), bf16),
            pltpu.VMEM((4 * ROWS, DEEP), bf16),
            pltpu.VMEM((512, 512), f32),
            pltpu.VMEM((64, 2048), f32),
            pltpu.VMEM((3, 16, 2048), f32),
            pltpu.VMEM((64, 512), f32),
            pltpu.VMEM((3, 16, 512), f32),
            pltpu.VMEM((16, 512), f32),
            pltpu.VMEM((ROWS, BATCH), f32),
            pltpu.VMEM((ITERS, 256, 128), f32),
            pltpu.VMEM((ITERS, 16, 128), f32),
            pltpu.VMEM((16, 128), f32),
            pltpu.VMEM((ROWS, BATCH), bf16),
            pltpu.SemaphoreType.REGULAR((9,)),
            pltpu.SemaphoreType.DMA((N_SEM,)),
            pltpu.SemaphoreType.DMA((N_SEM,)),
        ],
        compiler_params=pltpu.CompilerParams(
            collective_id=0, has_side_effects=True, vmem_limit_bytes=48 * 1024 * 1024
        ),
    )(noise.T, data.T)
    return targets.T, potential.reshape(BATCH)


def solution(mesh):
    in_specs = (P("batch", "group"), P("batch", "group"))
    out_specs = (P("batch", "group"), P())
    return jax.shard_map(local, mesh=mesh, in_specs=in_specs, out_specs=out_specs, check_vma=False)
```

time: 131 us -> 116 us (0.89)
  Pallas kernels: 124 us -> 112 us
    pallas_call x1, Pallas kernels: 124 us -> 112 us  [local(): pl.pallas_call(kernel, name='pairing', out_shape=(jax.ShapeDtypeStruct((W...]
where the time goes in v2:
time: 116 us
  Pallas kernels  112 us (97%)
  local copies, waits for them, and re-layouts  3.75 us (3%)
    pallas_call x1, Pallas kernels, local(): pl.pallas_call(kernel, name='pairing', out_shape=(jax.ShapeDtypeStruct((W...  112 us
    unnamed x6, local copies, waits for them, and re-layouts  3.75 us

profile of v2, /device:TPU:24, one launch (start us, length us, event | category | flops | bytes accessed | tf_op | source)
XLA Modules:
  0.0 115.9 jit_solution(5377443807905111812)
XLA Ops:
  0.6 0.0 copy-start
  0.6 1.1 copy-done
  1.8 0.0 copy-start.1
  1.8 1.1 copy-done.1
  2.9 111.5 %pairing.1 = (bf16[3120,128]{1,0:T(8,128)(2,1)S(1)}, f32[16,128]{1,0:T(8,128)S(1)}) custom-call(bf16[3120,128]{1,0:T(8,128)(2,1)S(1)} %bitcast.4, bf16[3120,128]{1,0:T(8,128)(2,1)S(1)} %bitcast.5), custom_call_target="tpu_custom_call" | custom-call | tf_op jit(solution)/shard_map/pairing/pallas_call | solution.py:404
  114.5 0.9 copy.6
  115.3 0.6 copy.7
Async XLA Ops:
  0.6 1.1 copy-start
  1.8 1.1 copy-start.1

commit v3 on v2

--- a/solution.py
+++ b/solution.py
@@ -17,6 +17,7 @@
 LOGA = np.float32(-np.log(np.float32(BATCH)))
 SCALE = np.float32(2.0 / (np.float64(FEAT) * np.float64(EPS)))
 A = ((0, 784), (784, 1168))
+AO = ((0, 656), (656, 656), (1312, 640))
 A_DEEP = 1952
 B = ((1952, 400), (2352, 400), (2752, 384))
 HALF = 1536
@@ -35,12 +36,10 @@
     return s + (s // 2) * (1 - 2 * (s % 2))
 
 
-def place(src_ref, dst, start, factor, own_at, const, const_at):
+def place(dst, start, factor, own_at, const, const_at):
     def chunk(k, total):
         at = pl.multiple_of(k * 240, 16)
-        piece = src_ref[pl.ds(at, 240)]
-        dst[pl.ds(pl.multiple_of(start + at, 16), 240)] = piece
-        piece = piece.astype(jnp.float32)
+        piece = dst[pl.ds(pl.multiple_of(start + at, 16), 240)].astype(jnp.float32)
         return total + jnp.sum((piece * piece).reshape(30, 8, ROWS), axis=0)
 
     total = lax.fori_loop(0, WIDE // 240, chunk, jnp.zeros((8, ROWS), jnp.float32))
@@ -55,12 +54,13 @@
 
 def kernel(
     noise_ref, data_ref, out_ref, pot_ref,
-    D, NT, Nr, C, R0, R1, S1, R2, F, M, L, lbuf, pbuf, W, known, send, recv,
+    D, NT, Nr, C, R0, R1, S1, R2, F, M, L, lbuf, pbuf, W, known, load, send, recv,
 ):
     b = lax.axis_index("batch")
     g = lax.axis_index("group")
     y, x, z, c = b // 4, b % 4, g // 2, g % 2
-    rho, s = z % 4, z // 4
+    rho, s = (z + 2) % 4, z // 4
+    hops = (6, 10, 2, 14)
 
     def dev(dy=0, dx=0, dz=0, dc=0):
         return (((y + dy) % 4) * 4 + (x + dx) % 4, ((z + dz) % 16) * 2 + (c + dc) % 2)
@@ -81,6 +81,14 @@
         started.append(copy)
         return copy
 
+    own = (x * 4 + y) * DEEP
+    loads = [
+        pltpu.make_async_copy(noise_ref, NT.at[pl.ds(0, WIDE)], load.at[0]),
+        pltpu.make_async_copy(data_ref, D.at[pl.ds(pl.multiple_of(own, 16), WIDE)], load.at[1]),
+    ]
+    for copy in loads:
+        copy.start()
+
     barrier = pltpu.get_barrier_semaphore()
     next_ones = (right, left, up, down, dev(dz=1), dev(dz=15), sibling)
     for device in next_ones:
@@ -102,8 +110,10 @@
     def nb(i, first, n):
         return NT.at[pl.ds(i * DEEP + first, n)]
 
-    place(noise_ref, NT, 0, -0.5, 0, -0.5, 3)
-    place(data_ref, D, (x * 4 + y) * DEEP, 1.0, 3, 1.0, 0)
+    loads[0].wait()
+    place(NT, 0, -0.5, 0, -0.5, 3)
+    loads[1].wait()
+    place(D, own, 1.0, 3, 1.0, 0)
     pl.semaphore_wait(barrier, len(next_ones))
 
     one, two = (0, HALF), (HALF, DEEP - HALF)
@@ -147,7 +157,8 @@
     hear(4)
     hear(5)
     hear(6, 3)
-    tell(7, dev(dz=4))
+    tell(7, dev(dz=2))
+    tell(8, dev(dz=14))
 
     a_r, a_l = {}, {}
     for piece in A:
@@ -247,7 +258,8 @@
     early_core = to_core(early)
     early_window = to_window(early_core, 0, 1152)
     hear(7)
-    tell(8, dev(dz=4), dev(dz=8), dev(dz=12))
+    hear(8)
+    tell(9, *(dev(dz=d) for d in hops))
     d_uo.wait_recv()
     d_do.wait_recv()
     cross(0, 3, 3, yo)
@@ -255,71 +267,56 @@
     flip(3, one)
     n_lo.wait_recv()
     flip(3, two)
-    for j, y_ in enumerate((y, yu, yd, yo)):
-        cross(3, 1, j, y_)
+    C[3 * ROWS :, :] = jnp.dot(
+        Nr[3 * ROWS :, :],
+        jnp.concatenate([D[rows(x, y_)] for y_ in (y, yu, yd, yo)], axis=1),
+        preferred_element_type=jnp.float32,
+    )
     rest_core = to_core(rest)
+    turn_a(A[0])
     add_window(early_window, early)
     rest_window = to_window(rest_core, 1152, 896)
-    turn_a(A[0])
     add_window(rest_window, rest)
-    stride = {}
-    for d in (2, 1, 3):
-        stride[d] = go(S1.at[sixteen(16 * ((s + d) % 4))], R2.at[d - 1], dev(dz=4 * d))
+    stride = [
+        go(S1.at[sixteen(16 * (((z + d) % 16) // 4))], R2.at[k], dev(dz=d)) for k, d in enumerate(hops)
+    ]
     turn_a(A[1])
     ao_r = go(blk(xl, y, 0, A_DEEP // 2), blk(xl, y, 0, A_DEEP // 2), right)
     ao_l = go(blk(xr, y, A_DEEP // 2, A_DEEP // 2), blk(xr, y, A_DEEP // 2, A_DEEP // 2), left)
-    hear(8, 3)
-    for d in (1, 2, 3):
-        stride[d].wait_recv()
-    F[...] = (S1[sixteen(16 * s)] + R2[0] + (R2[1] + R2[2])) * SCALE
+    hear(9, 4)
+    for copy in stride:
+        copy.wait_recv()
+    F[...] = ((R2[0] + R2[1]) + (R2[2] + R2[3])) * SCALE
 
     mine = sixteen(c * h + 16 * rho)
 
-    def part(x_):
-        return M.at[mine, pl.ds(pl.multiple_of(x_ * 512, 512), 512)]
-
-    dx = offset_of(s)
-    home = {}
-    for d in (2, 1, 3):
-        home[d] = go(F, part(x), dev(dx=dx, dz=4 * d))
-    home[0] = make(F, part(x), dev(dx=dx))
-
-    @pl.when(s != 0)
-    def _():
-        home[0].start()
-
-    @pl.when(s == 0)
-    def _():
-        M[mine, pl.ds(pl.multiple_of(x * 512, 512), 512)] = F[...]
+    def part(x_, at=None):
+        return M.at[mine if at is None else at, pl.ds(pl.multiple_of(x_ * 512, 512), 512)]
+
+    kept = sixteen(c * h + 16 * (z % 4))
+    home = [go(F, part(x, kept), dev(dx=offset_of(s), dz=d)) for d in hops]
 
     fwd_a("r", xr, A[0])
     fwd_a("l", xl, A[0])
     send_b("u", yu, "o", yo, *B)
     fwd_b("y", y, "d", yd, *B)
     spread, pair = {}, []
-    for d in (0, 1, 3, 2):
-        if d == 0:
-
-            @pl.when(s != 0)
-            def _():
-                home[0].wait_recv()
-
-        else:
-            home[d].wait_recv()
-        region = part((x + 4 - offset_of((s + 4 - d) % 4)) % 4)
+    for k in (2, 3, 0, 1):
+        home[k].wait_recv()
+        region = part((x + 4 - offset_of(((z + 16 - hops[k]) % 16) // 4)) % 4)
         for t, (_, device) in enumerate(steps):
-            spread[d, t] = go(region, region, device)
+            spread[k, t] = go(region, region, device)
         pair.append(go(region, region, sibling))
 
     send_b("d", yd, "y", y, B[0])
     ao_r.wait_recv()
     ao_l.wait_recv()
-    for piece in A:
-        send_a("o", xo, piece)
+    send_a("o", xo, AO[0])
+    fwd_a("r", xr, A[1])
 
     for t, dq in ((0, 3), (1, 1), (2, 2)):
-        for d in range(4):
-            spread[d, t].wait_recv()
+        for k in range(4):
+            spread[k, t].wait_recv()
         region = M.at[sixteen(c * h + 16 * ((rho + dq) % 4))]
         pair.append(go(region, region, sibling))
     for copy in pair:
@@ -327,17 +324,19 @@
 
     def between(step):
         if step == 0:
-            fwd_a("r", xr, A[1])
+            send_a("o", xo, AO[1])
             send_b("d", yd, "y", y, *B[1:])
         if step == 1:
-            fwd_a("l", xl, A[1])
+            send_a("o", xo, AO[2])
             send_b("o", yo, "u", yu, *B[:2])
         if step == 2:
-            fwd_a("o", xo, A[0])
+            fwd_a("l", xl, A[1])
+            fwd_a("o", xo, AO[0])
             send_b("o", yo, "u", yu, B[2])
             fwd_b("u", yu, "o", yo, B[0])
         if step == 3:
-            fwd_a("o", xo, A[1])
+            fwd_a("o", xo, AO[1])
+            fwd_a("o", xo, AO[2])
             fwd_b("u", yu, "o", yo, *B[1:])
 
     def block(k):
@@ -393,10 +392,6 @@
     for copy in started:
         copy.wait_send()
 
-    @pl.when(s != 0)
-    def _():
-        home[0].wait_send()
-
 
 def local(noise, data):
     f32, bf16 = jnp.float32, jnp.bfloat16
@@ -405,7 +400,7 @@
         kernel,
         name="pairing",
         out_shape=(jax.ShapeDtypeStruct((WIDE, ROWS), bf16), jax.ShapeDtypeStruct((16, ROWS), f32)),
-        in_specs=[vmem] * 2,
+        in_specs=[pl.BlockSpec(memory_space=pltpu.HBM)] * 2,
         out_specs=(vmem, vmem),
         scratch_shapes=[
             pltpu.VMEM((16 * DEEP, ROWS), bf16),
@@ -415,14 +410,15 @@
             pltpu.VMEM((64, 2048), f32),
             pltpu.VMEM((3, 16, 2048), f32),
             pltpu.VMEM((64, 512), f32),
-            pltpu.VMEM((3, 16, 512), f32),
+            pltpu.VMEM((4, 16, 512), f32),
             pltpu.VMEM((16, 512), f32),
             pltpu.VMEM((ROWS, BATCH), f32),
             pltpu.VMEM((ITERS, 256, 128), f32),
             pltpu.VMEM((ITERS, 16, 128), f32),
             pltpu.VMEM((16, 128), f32),
             pltpu.VMEM((ROWS, BATCH), bf16),
-            pltpu.SemaphoreType.REGULAR((9,)),
+            pltpu.SemaphoreType.REGULAR((10,)),
+            pltpu.SemaphoreType.DMA((2,)),
             pltpu.SemaphoreType.DMA((N_SEM,)),
             pltpu.SemaphoreType.DMA((N_SEM,)),
         ],

time: 116 us -> 114 us (0.983)
  Pallas kernels: 112 us -> 109 us
    pallas_call x1, Pallas kernels: 112 us -> 109 us  [local(): pl.pallas_call(kernel, name='pairing', out_shape=(jax.ShapeDtypeStruct((W...]
where the time goes in v3:
time: 114 us
  Pallas kernels  109 us (96%)
  local copies, waits for them, and re-layouts  3.75 us (3%)
    pallas_call x1, Pallas kernels, local(): pl.pallas_call(kernel, name='pairing', out_shape=(jax.ShapeDtypeStruct((W...  109 us
    unnamed x6, local copies, waits for them, and re-layouts  3.75 us

profile of v3, /device:TPU:24, one launch (start us, length us, event | category | flops | bytes accessed | tf_op | source)
XLA Modules:
  0.0 113.6 jit_solution(13794802650538991829)
XLA Ops:
  0.6 0.0 copy-start
  0.6 1.1 copy-done
  1.8 0.0 copy-start.1
  1.8 1.1 copy-done.1
  2.9 109.2 %pairing.1 = (bf16[3120,128]{1,0:T(8,128)(2,1)S(1)}, f32[16,128]{1,0:T(8,128)S(1)}) custom-call(bf16[3120,128]{1,0:T(8,128)(2,1)S(1)} %bitcast.4, bf16[3120,128]{1,0:T(8,128)(2,1)S(1)} %bitcast.5), custom_call_target="tpu_custom_call" | custom-call | tf_op jit(solution)/shard_map/pairing/pallas_call | solution.py:399
  112.1 0.9 copy.6
  113.0 0.6 copy.7
Async XLA Ops:
  0.6 1.1 %copy-start = (bf16[128,3120]{0,1:T(8,128)(2,1)S(1)}, bf16[128,3120]{0,1:T(8,128)(2,1)}, u32[]{:S(2)}) copy-start(bf16[128,3120]{0,1:T(8,128)(2,1)} %param.2) | copy-start | bytes 2396164
  1.8 1.1 %copy-start.1 = (bf16[128,3120]{0,1:T(8,128)(2,1)S(1)}, bf16[128,3120]{0,1:T(8,128)(2,1)}, u32[]{:S(2)}) copy-start(bf16[128,3120]{0,1:T(8,128)(2,1)} %param.3) | copy-start | bytes 2396164

commit v4 on v3

--- a/solution.py
+++ b/solution.py
@@ -252,7 +252,7 @@
     cross(0, 3, 0, y)
     d_u1.wait_recv()
     d_d1.wait_recv()
-    send_b("y", y, "d", yd, *B)
+    send_b("y", y, "d", yd, *B[:2])
     cross(0, 3, 1, yu)
     cross(0, 3, 2, yd)
     early_core = to_core(early)
@@ -283,6 +283,7 @@
     turn_a(A[1])
     ao_r = go(blk(xl, y, 0, A_DEEP // 2), blk(xl, y, 0, A_DEEP // 2), right)
     ao_l = go(blk(xr, y, A_DEEP // 2, A_DEEP // 2), blk(xr, y, A_DEEP // 2, A_DEEP // 2), left)
+    send_b("y", y, "d", yd, B[2])
     hear(9, 4)
     for copy in stride:
         copy.wait_recv()

time: 114 us -> 114 us (level)
  no operation moved by 1% of the time
where the time goes in v4:
time: 114 us
  Pallas kernels  109 us (96%)
  local copies, waits for them, and re-layouts  3.75 us (3%)
    pallas_call x1, Pallas kernels, local(): pl.pallas_call(kernel, name='pairing', out_shape=(jax.ShapeDtypeStruct((W...  109 us
    unnamed x6, local copies, waits for them, and re-layouts  3.75 us

profile of v4, /device:TPU:24, one launch (start us, length us, event | category | flops | bytes accessed | tf_op | source)
XLA Modules:
  0.0 113.6 jit_solution(13535170152549314976)
XLA Ops:
  0.6 0.0 copy-start
  0.6 1.1 copy-done
  1.8 0.0 copy-start.1
  1.8 1.1 copy-done.1
  2.9 109.2 %pairing.1 = (bf16[3120,128]{1,0:T(8,128)(2,1)S(1)}, f32[16,128]{1,0:T(8,128)S(1)}) custom-call(bf16[3120,128]{1,0:T(8,128)(2,1)S(1)} %bitcast.4, bf16[3120,128]{1,0:T(8,128)(2,1)S(1)} %bitcast.5), custom_call_target="tpu_custom_call" | custom-call | tf_op jit(solution)/shard_map/pairing/pallas_call | solution.py:400
  112.1 0.9 copy.6
  113.0 0.6 copy.7
Async XLA Ops:
  0.6 1.1 %copy-start = (bf16[128,3120]{0,1:T(8,128)(2,1)S(1)}, bf16[128,3120]{0,1:T(8,128)(2,1)}, u32[]{:S(2)}) copy-start(bf16[128,3120]{0,1:T(8,128)(2,1)} %param.2) | copy-start | bytes 2396164
  1.8 1.1 %copy-start.1 = (bf16[128,3120]{0,1:T(8,128)(2,1)S(1)}, bf16[128,3120]{0,1:T(8,128)(2,1)}, u32[]{:S(2)}) copy-start(bf16[128,3120]{0,1:T(8,128)(2,1)} %param.3) | copy-start | bytes 2396164
